TPU v7x, 256 devices: a whole 4x4x8 slice. The times are simulated.
256 devices in a mesh: seq: 16 (over z, core), fsdp: 16 (over x, y).
Axes of the slice: x: 4, y: 4, z: 8, core: 2. Of those that a mesh axis runs over, the one named last changes fastest.
Arguments:
- tokens: bfloat16 [16, 2048, 4096], P('fsdp', 'seq'), may hold values from -6 to 6
- queries: bfloat16 [16, 2048, 4096], P('fsdp', 'seq'), may hold values from -300 to 300, as said below
- norm_gain: float32 [4096], replicated, may hold values from 0.5 to 2
- w_key: bfloat16 [4096, 1024], P('fsdp'), may hold values from -0.09375 to 0.09375
- w_value: bfloat16 [4096, 1024], P('fsdp'), may hold values from -0.09375 to 0.09375
- block_list: int32 [16, 32, 32, 16], P('fsdp'), may hold values from -1 to 31, as said below
Outputs:
- attended: bfloat16 [16, 2048, 4096], P('fsdp', 'seq')
Inputs may be any that keep to these rules, and one draw needn't show every extreme that they name: `queries`: values at most a few hundred in magnitude. `block_list`: in every row the entries that are not -1 come first; they are distinct key blocks no later than the row's query block, and the query block itself is among them. Each row lists at least min(2, its query block + 1) blocks, and in every sequence some row lists 16.
All inputs are finite; a program needn't handle non-finite values.
Results may differ from a plain program's by a relative error of at most 0.015.
The roundings to bfloat16 on the way count: a program that leaves them out, or rounds other values in their place, can miss the bound.
Values may be sent and summed in bfloat16 or wider, within the bound.
A program may use at most 128 MiB of HBM per device.

v0:
```python
import math

import jax
import jax.numpy as jnp
from jax import lax
from jax.sharding import PartitionSpec as P

KV_HEADS = 8
HEAD_DIM = 128


EPS = 1e-05
ROPE_BASE = 500000.0


def rotary(values, positions):
    width = values.shape[-1]
    half_width = width // 2
    freqs = ROPE_BASE ** (-jnp.arange(half_width, dtype=jnp.float32) * (2.0 / width))
    angles = positions.astype(jnp.float32)[:, None] * freqs[None, :]
    cosine = jnp.cos(angles)[:, None, :]
    sine = jnp.sin(angles)[:, None, :]
    first = values[..., :half_width]
    second = values[..., half_width:]
    return jnp.concatenate(
        [first * cosine - second * sine, second * cosine + first * sine], axis=-1
    )


def attend_owner(owner_q, owner_k, owner_v, lists):
    per_owner, block_count, slot_count = lists.shape
    length, head_dim = owner_k.shape
    block_rows = length // block_count
    group_blocks = 8
    group_count = block_count // group_blocks
    query_groups = owner_q.reshape(group_count, group_blocks, block_rows, per_owner, head_dim)
    list_groups = lists.reshape(per_owner, group_count, group_blocks, slot_count).transpose(
        1, 0, 2, 3
    )
    key_tiles = owner_k.reshape(block_count, block_rows, head_dim)
    value_tiles = owner_v.reshape(block_count, block_rows, head_dim)
    score_scale = 1.0 / math.sqrt(head_dim)

    def attend_group(packed):
        query_part, list_part, group_pos = packed
        live_count = jnp.max(jnp.sum((list_part >= 0).astype(jnp.int32), axis=-1))
        query_pos = (group_pos * group_blocks + jnp.arange(group_blocks, dtype=jnp.int32))[
            :, None
        ] * block_rows + jnp.arange(block_rows, dtype=jnp.int32)[None, :]

        def score_slot(slot, buffer):
            slot_ids = lax.dynamic_index_in_dim(list_part, slot, axis=2, keepdims=False)
            block_ids = jnp.maximum(slot_ids, 0)
            key_part = key_tiles[block_ids]
            slot_scores = (
                jnp.einsum(
                    "qbpd,pqkd->pqbk", query_part, key_part, preferred_element_type=jnp.float32
                )
                * score_scale
            )
            key_pos = block_ids[..., None] * block_rows + jnp.arange(block_rows, dtype=jnp.int32)
            allowed = (slot_ids >= 0)[:, :, None, None] & (
                key_pos[:, :, None, :] <= query_pos[None, :, :, None]
            )
            slot_scores = jnp.where(allowed, slot_scores, -jnp.inf)
            return lax.dynamic_update_slice_in_dim(buffer, slot_scores, slot * block_rows, 3)

        empty_scores = jnp.full(
            (per_owner, group_blocks, block_rows, slot_count * block_rows), -jnp.inf, jnp.float32
        )
        scores = lax.fori_loop(0, live_count, score_slot, empty_scores)
        row_max = jnp.max(scores, axis=-1, keepdims=True)
        weights_raw = jnp.exp(scores - row_max)
        probs = (weights_raw / jnp.sum(weights_raw, axis=-1, keepdims=True)).astype(jnp.bfloat16)

        def value_slot(slot, total):
            slot_ids = lax.dynamic_index_in_dim(list_part, slot, axis=2, keepdims=False)
            value_part = value_tiles[jnp.maximum(slot_ids, 0)]
            prob_part = lax.dynamic_slice_in_dim(probs, slot * block_rows, block_rows, 3)
            return total + jnp.einsum(
                "pqbk,pqkd->qbpd", prob_part, value_part, preferred_element_type=jnp.float32
            )

        empty_total = jnp.zeros((group_blocks, block_rows, per_owner, head_dim), jnp.float32)
        output = lax.fori_loop(0, live_count, value_slot, empty_total)
        return output.astype(jnp.bfloat16)

    outputs = lax.map(
        attend_group, (query_groups, list_groups, jnp.arange(group_count, dtype=jnp.int32))
    )
    return outputs.reshape(length, per_owner * head_dim)


def on_device(tokens, queries, norm_gain, w_key, w_value, block_list):
    tok_rows = tokens.shape[1]
    seq_count = lax.axis_size("seq")
    seq_index = lax.axis_index("seq")
    head_count = block_list.shape[1]
    head_dim = HEAD_DIM
    kv_heads = KV_HEADS
    replicas = seq_count // kv_heads
    per_owner = head_count // seq_count
    positions = seq_index * tok_rows + jnp.arange(tok_rows, dtype=jnp.int32)
    wide = tokens[0].astype(jnp.float32)
    normed = (
        wide * lax.rsqrt(jnp.mean(wide * wide, axis=-1, keepdims=True) + EPS) * norm_gain
    ).astype(jnp.bfloat16)
    rotated = rotary(
        queries[0].astype(jnp.float32).reshape(tok_rows, head_count, head_dim), positions
    ).astype(jnp.bfloat16)
    patterns = block_list[0]
    sent_q = rotated.reshape(tok_rows, head_count * head_dim)
    my_lists = lax.dynamic_slice_in_dim(patterns, seq_index * per_owner, per_owner, 0)
    owner_q = lax.all_to_all(sent_q, "seq", split_axis=1, concat_axis=0, tiled=True)
    key_proj = jnp.dot(
        normed,
        lax.all_gather(w_key, "fsdp", axis=0, tiled=True),
        preferred_element_type=jnp.float32,
    )
    value_proj = jnp.dot(
        normed,
        lax.all_gather(w_value, "fsdp", axis=0, tiled=True),
        preferred_element_type=jnp.float32,
    )
    key_rows = rotary(key_proj.reshape(tok_rows, kv_heads, head_dim), positions).astype(
        jnp.bfloat16
    )
    value_rows = value_proj.astype(jnp.bfloat16)
    repeated_k = jnp.repeat(key_rows, replicas, axis=1).reshape(tok_rows, seq_count * head_dim)
    repeated_v = jnp.repeat(
        value_rows.reshape(tok_rows, kv_heads, head_dim), replicas, axis=1
    ).reshape(tok_rows, seq_count * head_dim)
    owner_k, owner_v = (
        lax.all_to_all(repeated_k, "seq", split_axis=1, concat_axis=0, tiled=True),
        lax.all_to_all(repeated_v, "seq", split_axis=1, concat_axis=0, tiled=True),
    )
    attended_owner = attend_owner(owner_q, owner_k, owner_v, my_lists)
    returned = lax.all_to_all(attended_owner, "seq", split_axis=0, concat_axis=1, tiled=True)
    return returned[None]


def solution(mesh):
    in_specs = (
        P("fsdp", "seq", None),
        P("fsdp", "seq", None),
        P(),
        P("fsdp", None),
        P("fsdp", None),
        P("fsdp", None, None, None),
    )
    out_specs = P("fsdp", "seq", None)
    return jax.shard_map(
        on_device, mesh=mesh, in_specs=in_specs, out_specs=out_specs, check_vma=False
    )
```

profile of v0, /device:TPU:193, one launch (start us, length us, event | category | flops | bytes accessed | tf_op | source)
XLA Modules:
  0.0 760.7 jit_solution(9877170169005644311)
XLA Ops:
  11.1 6.6 all-to-all-start
  18.0 68.3 %all-gather.3.cloned.1.call-done = bf16[4096,1024]{1,0:T(8,128)(2,1)} async-done(((bf16[256,1024]{1,0:T(8,128)(2,1)}), bf16[4096,1024]{1,0:T(8,128)(2,1)}) %all-gather.3.cloned.1.call-update) | async-done | bytes 8388624 | tf_op jit(solution)/shard_map/all_gather | solution.py:117
  86.4 11.2 %copy.43 = bf16[1024,4096]{1,0:T(8,128)(2,1)} copy(bf16[1024,4096]{0,1:T(8,128)(2,1)} %bitcast.104) | data formatting | bytes 16777216 | tf_op jit(solution)/shard_map/dot_general | solution.py:115
  97.6 5.8 fusion.20
  104.6 7.4 all-to-all-start.1
  112.1 52.3 %all-gather.5.cloned.1.call-done = bf16[4096,1024]{1,0:T(8,128)(2,1)} async-done(((bf16[256,1024]{1,0:T(8,128)(2,1)}), bf16[4096,1024]{1,0:T(8,128)(2,1)}) %all-gather.5.cloned.1.call-update) | async-done | bytes 8388624 | tf_op jit(solution)/shard_map/all_gather | solution.py:122
  164.3 4.7 fusion.18
  170.0 7.4 all-to-all-start.2
  180.1 11.4 %all-to-all-done.2 = bf16[128,16,128]{2,0,1:T(8,128)(2,1)S(1)} async-done(((bf16[128,16,128]{2,0,1:T(8,128)(2,1)}), bf16[128,16,128]{2,0,1:T(8,128)(2,1)S(1)}, u32[]{:S(2)}, u32[]{:S(2)}) %all-to-all-start.2) | async-done | bytes 524320 | tf_op jit(solution)/shard_map/all_to_all | solution.py:135
  191.5 480.0 %while.33 = (s32[]{:T(128)}, bf16[4,8,64,2,128]{4,3,2,1,0:T(2,128)(2,1)}, s32[4,2,8,16]{3,2,0,1:T(8,128)S(1)}, bf16[4,8,64,2,128]{4,3,2,1,0:T(2,128)(2,1)S(1)}, ...) while((s32[]{:T(128)}, ...), condition=%wide.region_10.11_spmd, body=%wide.region_1.10_spmd.sunk | while | flops 37232984 | bytes 17329664 | solution.py:88
  196.2 49.0 %while.34 = (s32[]{:T(128)}, f32[2,8,64,1024]{3,2,1,0:T(8,128)}, s32[]{:T(128)}, s32[2,8,16]{1,0,2:T(2,128)S(1)}, bf16[32,64,128]{2,1,0:T(8,128)(2,1)S(1)}, /*in...) while((s32[]{:T(128)}, f32[2,8,64,1024]{3,2,1,0:T(8,128)}, ...), condition=%wide.region_5.5_spmd.clone, body=%wide.region_4.4_spmd.clone.sunk | while | flops 17041972 | bytes 1852241 | solution.py:71
  197.9 3.6 dynamic_update_slice.12
  203.2 5.1 dynamic_update_slice.12
  210.0 3.6 dynamic_update_slice.12
  215.3 5.1 dynamic_update_slice.12
  222.2 3.5 dynamic_update_slice.12
  227.4 5.1 dynamic_update_slice.12
  239.5 5.1 dynamic_update_slice.12
  245.2 5.7 divide_convert_fusion.2
  250.9 20.9 %while.35 = (s32[]{:T(128)}, f32[8,64,2,128]{3,1,2,0:T(8,128)S(1)}, s32[]{:T(128)}, s32[2,8,16]{1,0,2:T(2,128)S(1)}, bf16[32,64,128]{2,1,0:T(8,128)(2,1)S(1)}, /...) while((s32[]{:T(128)}, f32[8,64,2,128]{3,1,2,0:T(8,128)S(1)}, ...), condition=%wide.region_9.9_spmd, body=%wide.region_8.8_spmd.sunk | while | flops 16909336 | bytes 2101829 | solution.py:85
  277.5 85.3 %while.34 = (s32[]{:T(128)}, f32[2,8,64,1024]{3,2,1,0:T(8,128)}, s32[]{:T(128)}, s32[2,8,16]{1,0,2:T(2,128)S(1)}, bf16[32,64,128]{2,1,0:T(8,128)(2,1)S(1)}, /*in...) while((s32[]{:T(128)}, f32[2,8,64,1024]{3,2,1,0:T(8,128)}, ...), condition=%wide.region_5.5_spmd.clone, body=%wide.region_4.4_spmd.clone.sunk | while | flops 17041972 | bytes 1852241 | solution.py:71
  279.2 3.6 dynamic_update_slice.12
  284.5 5.1 dynamic_update_slice.12
  291.4 3.6 dynamic_update_slice.12
  296.7 5.1 dynamic_update_slice.12
  303.5 3.5 dynamic_update_slice.12
  308.8 5.1 dynamic_update_slice.12
  320.8 5.1 dynamic_update_slice.12
  327.7 3.6 dynamic_update_slice.12
  333.0 5.1 dynamic_update_slice.12
  339.8 3.5 dynamic_update_slice.12
  345.1 5.1 dynamic_update_slice.12
  357.1 5.1 dynamic_update_slice.12
  362.8 5.7 divide_convert_fusion.2
  368.6 36.1 %while.35 = (s32[]{:T(128)}, f32[8,64,2,128]{3,1,2,0:T(8,128)S(1)}, s32[]{:T(128)}, s32[2,8,16]{1,0,2:T(2,128)S(1)}, bf16[32,64,128]{2,1,0:T(8,128)(2,1)S(1)}, /...) while((s32[]{:T(128)}, f32[8,64,2,128]{3,1,2,0:T(8,128)S(1)}, ...), condition=%wide.region_9.9_spmd, body=%wide.region_8.8_spmd.sunk | while | flops 16909336 | bytes 2101829 | solution.py:85
  410.4 85.3 %while.34 = (s32[]{:T(128)}, f32[2,8,64,1024]{3,2,1,0:T(8,128)}, s32[]{:T(128)}, s32[2,8,16]{1,0,2:T(2,128)S(1)}, bf16[32,64,128]{2,1,0:T(8,128)(2,1)S(1)}, /*in...) while((s32[]{:T(128)}, f32[2,8,64,1024]{3,2,1,0:T(8,128)}, ...), condition=%wide.region_5.5_spmd.clone, body=%wide.region_4.4_spmd.clone.sunk | while | flops 17041972 | bytes 1852241 | solution.py:71
  412.1 3.6 dynamic_update_slice.12
  417.4 5.1 dynamic_update_slice.12
  424.3 3.6 dynamic_update_slice.12
  429.6 5.1 dynamic_update_slice.12
  436.4 3.5 dynamic_update_slice.12
  441.7 5.1 dynamic_update_slice.12
  453.7 5.1 dynamic_update_slice.12
  460.6 3.6 dynamic_update_slice.12
  465.8 5.1 dynamic_update_slice.12
  477.9 5.1 dynamic_update_slice.12
  490.0 5.1 dynamic_update_slice.12
  495.7 5.7 divide_convert_fusion.2
  501.5 36.1 %while.35 = (s32[]{:T(128)}, f32[8,64,2,128]{3,1,2,0:T(8,128)S(1)}, s32[]{:T(128)}, s32[2,8,16]{1,0,2:T(2,128)S(1)}, bf16[32,64,128]{2,1,0:T(8,128)(2,1)S(1)}, /...) while((s32[]{:T(128)}, f32[8,64,2,128]{3,1,2,0:T(8,128)S(1)}, ...), condition=%wide.region_9.9_spmd, body=%wide.region_8.8_spmd.sunk | while | flops 16909336 | bytes 2101829 | solution.py:85
  543.3 85.3 %while.34 = (s32[]{:T(128)}, f32[2,8,64,1024]{3,2,1,0:T(8,128)}, s32[]{:T(128)}, s32[2,8,16]{1,0,2:T(2,128)S(1)}, bf16[32,64,128]{2,1,0:T(8,128)(2,1)S(1)}, /*in...) while((s32[]{:T(128)}, f32[2,8,64,1024]{3,2,1,0:T(8,128)}, ...), condition=%wide.region_5.5_spmd.clone, body=%wide.region_4.4_spmd.clone.sunk | while | flops 17041972 | bytes 1852241 | solution.py:71
  545.0 3.6 dynamic_update_slice.12
  550.3 5.1 dynamic_update_slice.12
  557.2 3.6 dynamic_update_slice.12
  562.5 5.1 dynamic_update_slice.12
  569.3 3.5 dynamic_update_slice.12
  574.6 5.1 dynamic_update_slice.12
  586.6 5.1 dynamic_update_slice.12
  593.4 3.6 dynamic_update_slice.12
  598.7 5.1 dynamic_update_slice.12
  610.8 5.1 dynamic_update_slice.12
  622.9 5.1 dynamic_update_slice.12
  628.6 5.7 divide_convert_fusion.2
  634.4 36.1 %while.35 = (s32[]{:T(128)}, f32[8,64,2,128]{3,1,2,0:T(8,128)S(1)}, s32[]{:T(128)}, s32[2,8,16]{1,0,2:T(2,128)S(1)}, bf16[32,64,128]{2,1,0:T(8,128)(2,1)S(1)}, /...) while((s32[]{:T(128)}, f32[8,64,2,128]{3,1,2,0:T(8,128)S(1)}, ...), condition=%wide.region_9.9_spmd, body=%wide.region_8.8_spmd.sunk | while | flops 16909336 | bytes 2101829 | solution.py:85
  673.3 78.6 %all_to_all.61 = bf16[16,128,256]{2,1,0:T(8,128)(2,1)S(1)} all-to-all(bf16[16,128,256]{2,1,0:T(8,128)(2,1)S(1)} %all_to_all.54), channel_id=1, replica_groups=mesh['seq'=16,'fsdp'=16] {'seq'}, dimensions={0} | all-to-all | bytes 2097152 | tf_op jit(solution)/shard_map/all_to_all | solution.py:138
  (742 shorter events, 218.5 us)
Async XLA Ops:
  6.5 170.8 %copy-start = (s32[1,32,32,16]{2,3,1,0:T(8,128)S(1)}, s32[1,32,32,16]{2,3,1,0:T(8,128)}, u32[]{:S(2)}) copy-start(s32[1,32,32,16]{2,3,1,0:T(8,128)} %param.17) | copy-start | bytes 196612
  6.5 79.8 %all-gather.3.cloned.1.call-start = ((), (), s32[]{:S(2)}) async-start(), calls=%async_computation.4 | async-start | bytes 8912896 | tf_op jit(solution)/shard_map/all_gather | solution.py:117
  7.3 157.1 %all-gather.5.cloned.1.call-start = ((), (), s32[]{:S(2)}) async-start(), calls=%async_computation.5 | async-start | bytes 8912896 | tf_op jit(solution)/shard_map/all_gather | solution.py:122
  9.5 8.3 %copy-start.1 = (bf16[1,128,4096]{2,1,0:T(8,128)(2,1)S(1)}, bf16[1,128,4096]{2,1,0:T(8,128)(2,1)}, u32[]{:S(2)}) copy-start(bf16[1,128,4096]{2,1,0:T(8,128)(2,1)} %param.12) | copy-start | bytes 3145732
  11.1 92.6 %all-to-all-start = ((bf16[128,16,256]{0,2,1:T(8,128)(2,1)}), bf16[128,16,256]{0,2,1:T(8,128)(2,1)S(1)}, u32[]{:S(2)}, u32[]{:S(2)}) async-start(bf16[128,16,256]{0,2,1:T(8,128)(2,1)} %bitcast.9), calls=%async_computation | async-start | bytes 2097152 | tf_op jit(solution)/shard_map/all_to_all | solution.py:114
  86.4 11.2 %copy-start.2 = (f32[4096]{0:T(1024)S(1)}, f32[4096]{0:T(1024)}, u32[]{:S(2)}) copy-start(f32[4096]{0:T(1024)} %param.14) | copy-start | bytes 49156
  104.6 64.5 %all-to-all-start.1 = ((bf16[128,16,128]{2,0,1:T(8,128)(2,1)}), bf16[128,16,128]{2,0,1:T(8,128)(2,1)S(1)}, u32[]{:S(2)}, u32[]{:S(2)}) async-start(bf16[128,16,128]{2,0,1:T(8,128)(2,1)} %bitcast.16), calls=%async_computation.1 | async-start | bytes 1048576 | tf_op jit(solution)/shard_map/all_to_all | solution.py:134
  170.0 21.5 %all-to-all-start.2 = ((bf16[128,16,128]{2,0,1:T(8,128)(2,1)}), bf16[128,16,128]{2,0,1:T(8,128)(2,1)S(1)}, u32[]{:S(2)}, u32[]{:S(2)}) async-start(bf16[128,16,128]{2,0,1:T(8,128)(2,1)} %bitcast.19), calls=%async_computation.2 | async-start | bytes 1048576 | tf_op jit(solution)/shard_map/all_to_all | solution.py:135
Sparse Core Ops, SparseCore 0:
  9.8 76.5 all-gather.2
  88.8 75.4 all-gather.4
where the time goes:
time: 774 us; the launch traced here: 761 us
  local copies, waits for them, and re-layouts  323 us (42%)
  waiting for transfers between devices  133 us (17%)
  matrix products  86.6 us (11%)
  blocking collectives  78.6 us (10%)
  loops' own time  67.1 us (9%)
  other arithmetic  36.8 us (5%)
  starting transfers between devices  21.5 us (3%)
  between operations  13.6 us (2%)
    dynamic_update_slice x50, local copies, waits for them, and re-layouts, score_slot(): lax.dynamic_update_slice_in_dim(buffer, slot_scores, slot * block_rows, 3)  217 us
    all_to_all x1, blocking collectives, on_device(): lax.all_to_all(attended_owner, 'seq', split_axis=0, concat_axis=1, tiled=...  78.6 us
    all_gather x1, waiting for transfers between devices, on_device(): lax.all_gather(w_key, 'fsdp', axis=0, tiled=True)  68.3 us
    dot_general x50, matrix products, value_slot(): jnp.einsum('pqbk,pqkd->qbpd', prob_part, value_part, preferred_element_ty...  62.3 us
    all_gather x1, waiting for transfers between devices, on_device(): lax.all_gather(w_value, 'fsdp', axis=0, tiled=True)  52.3 us
    another operation x4, loops' own time, attend_group(): scores = lax.fori_loop(0, live_count, score_slot, empty_scores)  32.4 us
    another operation x4, loops' own time, attend_group(): output = lax.fori_loop(0, live_count, value_slot, empty_total)  32 us
    gather x50, local copies, waits for them, and re-layouts, score_slot(): key_part = key_tiles[block_ids]  29.8 us
  transfers between devices with their start and end apart: 5, of which 3 were waited for; matrix products, arithmetic and copies ran while one was open for 4% of the time, Pallas kernels for 0%

commit v1 on v0

v1 whole, which is shorter than its diff:
```python
import functools
import math

import jax
import jax.numpy as jnp
import numpy as np
from jax import lax
from jax.experimental import pallas as pl
from jax.experimental.pallas import tpu as pltpu
from jax.sharding import PartitionSpec as P

MESH = pl.DeviceIdType.MESH
EPS = 1e-05
ROPE_BASE = 500000.0
D = 4096
HD = 128
LENGTH = 2048
NX, NY, NZ = 4, 4, 8
KVL = 4
GROUP = 4
CHUNKS = 2 * KVL
ROWS = 128
PAIR = 2 * ROWS
BLOCK = 64
QB = PAIR // BLOCK
HIDDEN = -1e30
SCALE = math.log2(math.e) / math.sqrt(HD)


def rotary_tables():
    freqs = np.float32(ROPE_BASE) ** (
        -np.arange(HD // 2, dtype=np.float32) * np.float32(2.0 / HD)
    )
    angles = np.arange(LENGTH, dtype=np.float32)[:, None] * freqs.astype(np.float32)[None, :]
    cosine = np.cos(angles.astype(np.float64)).astype(np.float32)
    sine = np.sin(angles.astype(np.float64)).astype(np.float32)
    return np.concatenate([cosine, cosine], 1), np.concatenate([-sine, sine], 1)


def kernel(
    tokens, queries, gain, wk, wv, lists, cos_hbm, sin_hbm, out,
    wbuf, nrm, tok, gn, qin, qrot, qsend, kv, cs, sn, lst, bias, tri, sbuf, obuf,
    in_sem, own_sem, wsend, wrecv, zsend, zrecv, core_send, core_recv, osend, orecv, olocal,
):
    s = lax.axis_index("seq")
    f = lax.axis_index("fsdp")
    c = lax.rem(s, 2)
    z = lax.div(s, 2)
    x = lax.div(f, NY)
    y = lax.rem(f, NY)
    xn, xp = lax.rem(x + NX - 1, NX), lax.rem(x + 1, NX)
    yn, yp = lax.rem(y + NY - 1, NY), lax.rem(y + 1, NY)
    x2, y2 = lax.rem(x + 2, NX), lax.rem(y + 2, NY)
    x_dev = ((s, xp * NY + y), (s, xn * NY + y))
    y_dev = ((s, x * NY + yp), (s, x * NY + yn))
    z_dev = ((lax.rem(s + 2, 2 * NZ), f), (lax.rem(s + 2 * NZ - 2, 2 * NZ), f))
    partner = (s + 1 - 2 * c, f)
    row0 = pl.multiple_of(c * ROWS, ROWS)
    row1 = pl.multiple_of((1 - c) * ROWS, ROWS)

    def own_copy(t):
        kvl = lax.div(t, 2)
        cols = pl.ds(pl.multiple_of((KVL * c + kvl) * HD, HD), HD)
        return [
            pltpu.make_async_copy(w.at[:, :, cols], wbuf.at[t, x, y], own_sem.at[t])
            for w in (wk, wv)
        ]

    def start_own(t):
        key_copy, value_copy = own_copy(t)

        @pl.when(lax.rem(t, 2) == 0)
        def _():
            key_copy.start()

        @pl.when(lax.rem(t, 2) == 1)
        def _():
            value_copy.start()

    pos = pl.ds(pl.multiple_of(z * PAIR, PAIR), PAIR)
    tok_copy = pltpu.make_async_copy(tokens, tok, in_sem.at[0])
    gain_copy = pltpu.make_async_copy(gain, gn, in_sem.at[1])
    q_copy = pltpu.make_async_copy(queries, qin, in_sem.at[2])
    cos_copy = pltpu.make_async_copy(cos_hbm.at[pos, :], cs.at[0], in_sem.at[3])
    sin_copy = pltpu.make_async_copy(sin_hbm.at[pos, :], sn.at[0], in_sem.at[4])
    list_copy = pltpu.make_async_copy(lists, lst, in_sem.at[5])

    start_own(0)
    start_own(1)
    tok_copy.start()
    gain_copy.start()
    cos_copy.start()
    sin_copy.start()
    q_copy.start()
    list_copy.start()
    for t in range(2, CHUNKS):
        start_own(t)

    barrier = pltpu.get_barrier_semaphore()
    for device in (*x_dev, *y_dev, *z_dev, partner):
        pl.semaphore_signal(barrier, inc=1, device_id=device, device_id_type=MESH)
    pl.semaphore_wait(barrier, 7)

    def remote(src, dst, send, recv, device):
        return pltpu.make_async_remote_copy(
            src_ref=src, dst_ref=dst, send_sem=send, recv_sem=recv, device_id=device, device_id_type=MESH
        )

    first_dev = (x_dev, y_dev)
    second_dev = (y_dev, x_dev)

    def piece(t, half, step):
        if half == 0:
            return wbuf.at[t, (x, xn, x2, xp)[step], y, 0]
        return wbuf.at[t, x, (y, yn, y2, yp)[step], 1]

    def line(t, half, step, part=None):
        some = pl.ds(0, 4) if part is None else pl.ds(2 * part, 2)
        if half == 0:
            return wbuf.at[t, some, (y, yn, y2, yp)[step], 0]
        return wbuf.at[t, (x, xn, x2, xp)[step], some, 1]

    def rows_of(ref, part):
        return ref.at[pl.ds(64 * part, 64), :]

    def w_send(t, stage, half, d, ref, device):
        remote(ref, ref, wsend.at[t], wrecv.at[t, stage, half, d], device).start()

    def w_wait(t, stage, half, d, ref):
        remote(ref, ref, wsend.at[t], wrecv.at[t, stage, half, d], partner).wait_recv()

    def stage0(t):
        own_copy(t)[0].wait()
        for half in range(2):
            for d in range(2):
                w_send(t, 0, half, d, piece(t, half, 0), first_dev[half][d])

    def stage1(t):
        for half in range(2):
            for d, step in ((0, 1), (1, 3)):
                w_wait(t, 0, half, d, piece(t, half, step))
                w_send(t, 1, half, d, rows_of(piece(t, half, step), d), first_dev[half][d])

    def stage2(t):
        for half in range(2):
            for d in range(2):
                w_wait(t, 1, half, d, rows_of(piece(t, half, 2), d))
            for d in range(2):
                w_send(t, 2, half, d, line(t, half, 0), second_dev[half][d])

    def stage3(t):
        for half in range(2):
            for d, step in ((0, 1), (1, 3)):
                w_wait(t, 2, half, d, line(t, half, step))
                w_send(t, 3, half, d, line(t, half, step, d), second_dev[half][d])

    def stage4(t):
        for half in range(2):
            for d in range(2):
                w_wait(t, 3, half, d, line(t, half, 2, d))

    def z_slot(t, stage, d):
        if stage == 3:
            return kv.at[t, 4, pl.ds(128 * d, 128), :]
        return kv.at[t, stage + 1 if d == 0 else 7 - stage]

    def z_source(t, stage, d):
        if stage == 3:
            return kv.at[t, 3 if d == 0 else 5, pl.ds(128 * d, 128), :]
        return kv.at[t, stage if d == 0 else (8 - stage) % 8]

    def z_send(t, stage):
        for d in range(2):
            remote(
                z_source(t, stage, d), z_slot(t, stage, d), zsend.at[t], zrecv.at[t, stage, d], z_dev[d]
            ).start()

    def z_wait(t, stage):
        for d in range(2):
            ref = z_slot(t, stage, d)
            remote(ref, ref, zsend.at[t], zrecv.at[t, stage, d], partner).wait_recv()

    nrm_copy = remote(
        nrm.at[pl.ds(row0, ROWS), :], nrm.at[pl.ds(row0, ROWS), :], core_send.at[0], core_recv.at[0], partner
    )
    q_rot_copy = remote(
        qsend, qrot.at[:, :, pl.ds(row0, ROWS), :], core_send.at[1], core_recv.at[1], partner
    )
    nrm_landing = nrm.at[pl.ds(row1, ROWS), :]
    q_landing = qrot.at[:, :, pl.ds(row1, ROWS), :]

    def normalise():
        tok_copy.wait()
        gain_copy.wait()

        @pl.loop(0, ROWS // 16)
        def _(i):
            rows = pl.ds(pl.multiple_of(i * 16, 16), 16)
            wide = tok[rows, :].astype(jnp.float32)
            mean = jnp.sum(wide * wide, axis=-1, keepdims=True) * (1.0 / D)
            normed = wide * lax.rsqrt(mean + EPS) * gn[...]
            nrm[pl.ds(pl.multiple_of(row0 + i * 16, 16), 16), :] = normed.astype(jnp.bfloat16)

        nrm_copy.start()

    def rotate_queries():
        q_copy.wait()
        cos_copy.wait()
        sin_copy.wait()
        cs[1] = jnp.ones((PAIR, HD), jnp.float32)
        sn[1] = jnp.zeros((PAIR, HD), jnp.float32)

        def rotated(head):
            cols = pl.ds(pl.multiple_of(head * HD, HD), HD)
            v = qin[:, cols].astype(jnp.float32)
            turned = v * cs[0, pl.ds(row0, ROWS), :] + pltpu.roll(v, HD // 2, 1) * sn[0, pl.ds(row0, ROWS), :]
            return turned.astype(jnp.bfloat16)

        @pl.loop(0, KVL * GROUP)
        def _(h):
            kvl, g = lax.div(h, GROUP), lax.rem(h, GROUP)
            qsend[kvl, g] = rotated((1 - c) * KVL * GROUP + h)
            qrot[kvl, g, pl.ds(row0, ROWS), :] = rotated(c * KVL * GROUP + h)

        q_rot_copy.start()

    def make_bias():
        list_copy.wait()

        @pl.loop(0, NZ)
        def _(r):
            chip = lax.rem(z - r + NZ, NZ)
            blocks = lax.div(lax.broadcasted_iota(jnp.int32, (1, PAIR), 1), BLOCK) + chip * QB
            for n in range(KVL * GROUP * QB // 8):
                ids = lst[8 * n : 8 * n + 8, :]
                hit = ids[:, 0:1] == blocks
                for slot in range(1, ids.shape[1]):
                    hit = hit | (ids[:, slot : slot + 1] == blocks)
                bias[8 * n : 8 * n + 8, pl.ds(pl.multiple_of(r * PAIR, PAIR), PAIR)] = jnp.where(
                    hit, 0.0, HIDDEN
                )

        i = lax.broadcasted_iota(jnp.int32, (PAIR, PAIR), 0)
        j = lax.broadcasted_iota(jnp.int32, (PAIR, PAIR), 1)
        tri[...] = jnp.where(j <= i, 0.0, HIDDEN)

    def project(t):
        def step(k, acc):
            kx, ky = lax.div(k, 2), lax.rem(k, 2)
            w = wbuf[t, kx, pl.ds(2 * ky, 2)].reshape(512, HD)
            a = nrm[:, pl.ds(pl.multiple_of(k * 512, 512), 512)]
            return acc + jnp.dot(a, w, preferred_element_type=jnp.float32)

        acc = lax.fori_loop(0, 8, step, jnp.zeros((PAIR, HD), jnp.float32))
        kind = lax.rem(t, 2)
        kv[t, 0] = (acc * cs[kind] + pltpu.roll(acc, HD // 2, 1) * sn[kind]).astype(jnp.bfloat16)

    def attend(kvl, g):
        q = qrot[kvl, g]
        head = kvl * GROUP + g
        top = None
        for r in range(NZ):
            scores = lax.dot_general(
                q, kv[2 * kvl, r], (((1,), (1,)), ((), ())), preferred_element_type=jnp.float32
            )
            cols = slice(r * PAIR, (r + 1) * PAIR)
            hide = jnp.concatenate(
                [
                    jnp.broadcast_to(bias[pl.ds(head * QB + b, 1), cols], (BLOCK, PAIR))
                    for b in range(QB)
                ],
                0,
            )
            scores = scores * SCALE + hide
            if r == 0:
                scores = scores + tri[...]
            sbuf[:, cols] = scores
            here = jnp.maximum(scores[:, :HD], scores[:, HD:])
            top = here if top is None else jnp.maximum(top, here)
        top = jnp.max(top, axis=-1, keepdims=True)
        total, acc = None, None
        for r in range(NZ):
            p = jnp.exp2(sbuf[:, r * PAIR : (r + 1) * PAIR] - top)
            both = p[:, :HD] + p[:, HD:]
            total = both if total is None else total + both
            part = jnp.dot(p.astype(jnp.bfloat16), kv[2 * kvl + 1, r], preferred_element_type=jnp.float32)
            acc = part if acc is None else acc + part
        total = jnp.sum(total, axis=-1, keepdims=True)
        obuf[kvl, g] = (acc / total).astype(jnp.bfloat16)

    def out_cols(core, kvl, g):
        return out.at[:, pl.ds(pl.multiple_of(((core * KVL + kvl) * GROUP + g) * HD, HD), HD)]

    def out_local(kvl, g):
        return pltpu.make_async_copy(
            obuf.at[kvl, g, pl.ds(row0, ROWS), :], out_cols(c, kvl, g), olocal.at[kvl, g]
        )

    def out_remote(kvl, g):
        return remote(
            obuf.at[kvl, g, pl.ds(row1, ROWS), :], out_cols(c, kvl, g), osend.at[kvl, g], orecv.at[kvl, g], partner
        )

    def attend_and_send(kvl, g):
        attend(kvl, g)
        out_local(kvl, g).start()
        out_remote(kvl, g).start()

    stage0(jnp.int32(0))

    def slot(n, carry):
        def when(t, what, low=0, high=CHUNKS):
            @pl.when((t >= low) & (t < high))
            def _():
                what(t)

        when(n + 1, stage0)

        @pl.when(n == 0)
        def _():
            normalise()

        when(n, stage1)

        @pl.when(n == 0)
        def _():
            rotate_queries()

        def z1(t):
            z_wait(t, 0)
            z_send(t, 1)

        def z2(t):
            z_wait(t, 1)
            z_send(t, 2)

        def z3(t):
            z_wait(t, 2)
            z_send(t, 3)

        def unit(which):
            u = 2 * (n - 6) + which

            @pl.when((u >= 0) & (u < KVL * GROUP))
            def _():
                attend_and_send(lax.div(u, GROUP), lax.rem(u, GROUP))

        when(n - 4, z1)
        when(n - 1, stage2)
        when(n - 5, lambda t: z_wait(t, 3))
        unit(0)
        when(n - 4, z2)

        @pl.when(n == 1)
        def _():
            make_bias()

        when(n - 2, stage3)
        unit(1)
        when(n - 4, z3)

        @pl.when(n == 2)
        def _():
            remote(nrm_landing, nrm_landing, core_send.at[0], core_recv.at[0], partner).wait_recv()
            remote(q_landing, q_landing, core_send.at[1], core_recv.at[1], partner).wait_recv()

        def compute(t):
            stage4(t)
            project(t)
            z_send(t, 0)

        when(n - 3, compute)
        return carry

    lax.fori_loop(0, 14, slot, 0)

    nrm_copy.wait_send()
    q_rot_copy.wait_send()

    @pl.loop(0, CHUNKS)
    def _(t):
        sent = nrm.at[:, pl.ds(0, 15 * HD)]
        pltpu.make_async_copy(sent, sent, wsend.at[t]).wait()
        around = kv.at[t, pl.ds(0, 7)]
        pltpu.make_async_copy(around, around, zsend.at[t]).wait()

    @pl.loop(0, KVL * GROUP)
    def _(u):
        kvl, g = lax.div(u, GROUP), lax.rem(u, GROUP)
        out_local(kvl, g).wait()
        out_remote(kvl, g).wait_send()
        theirs = out_cols(1 - c, kvl, g)
        remote(theirs, theirs, osend.at[kvl, g], orecv.at[kvl, g], partner).wait_recv()


def on_device(tokens, queries, norm_gain, w_key, w_value, block_list):
    s = lax.axis_index("seq")
    c, z = lax.rem(s, 2), lax.div(s, 2)
    heads = KVL * GROUP
    lists = lax.dynamic_slice(block_list[0], (c * heads, z * QB, 0), (heads, QB, block_list.shape[3]))
    lists = lists.reshape(heads * QB, block_list.shape[3])
    cosine, sine = rotary_tables()
    bf16, f32 = jnp.bfloat16, jnp.float32
    dma = pltpu.SemaphoreType.DMA
    out = pl.pallas_call(
        kernel,
        name="layer",
        out_shape=jax.ShapeDtypeStruct((ROWS, D), bf16),
        in_specs=[pl.BlockSpec(memory_space=pl.ANY)] * 8,
        out_specs=pl.BlockSpec(memory_space=pl.ANY),
        scratch_shapes=[
            pltpu.VMEM((CHUNKS, NX, NY, 2, 128, HD), bf16),
            pltpu.VMEM((PAIR, D), bf16),
            pltpu.VMEM((ROWS, D), bf16),
            pltpu.VMEM((1, D), f32),
            pltpu.VMEM((ROWS, D), bf16),
            pltpu.VMEM((KVL, GROUP, PAIR, HD), bf16),
            pltpu.VMEM((KVL, GROUP, ROWS, HD), bf16),
            pltpu.VMEM((CHUNKS, NZ, PAIR, HD), bf16),
            pltpu.VMEM((2, PAIR, HD), f32),
            pltpu.VMEM((2, PAIR, HD), f32),
            pltpu.VMEM((heads * QB, block_list.shape[3]), jnp.int32),
            pltpu.VMEM((heads * QB, LENGTH), f32),
            pltpu.VMEM((PAIR, PAIR), f32),
            pltpu.VMEM((PAIR, LENGTH), f32),
            pltpu.VMEM((KVL, GROUP, PAIR, HD), bf16),
            dma((6,)),
            dma((CHUNKS,)),
            dma((CHUNKS,)),
            dma((CHUNKS, 4, 2, 2)),
            dma((CHUNKS,)),
            dma((CHUNKS, 4, 2)),
            dma((2,)),
            dma((2,)),
            dma((KVL, GROUP)),
            dma((KVL, GROUP)),
            dma((KVL, GROUP)),
        ],
        compiler_params=pltpu.CompilerParams(
            collective_id=0, has_side_effects=True, vmem_limit_bytes=56 * 2**20
        ),
        cost_estimate=pl.CostEstimate(
            flops=6_400_000_000, bytes_accessed=6_000_000, transcendentals=8_400_000
        ),
    )(
        tokens[0],
        queries[0],
        norm_gain[None],
        w_key.reshape(2, 128, w_key.shape[1]),
        w_value.reshape(2, 128, w_value.shape[1]),
        lists,
        jnp.asarray(cosine),
        jnp.asarray(sine),
    )
    return out[None]


def solution(mesh):
    in_specs = (
        P("fsdp", "seq", None),
        P("fsdp", "seq", None),
        P(),
        P("fsdp", None),
        P("fsdp", None),
        P("fsdp", None, None, None),
    )
    return jax.shard_map(
        on_device, mesh=mesh, in_specs=in_specs, out_specs=P("fsdp", "seq", None), check_vma=False
    )
```

time: 774 us -> 154 us (0.20)
  the two profiles are of different devices: /device:TPU:193 before, /device:TPU:1 now
where the time goes in v1:
time: 154 us
  Pallas kernels  150 us (97%)
  local copies, waits for them, and re-layouts  4.11 us (3%)
    pallas_call x1, Pallas kernels, on_device(): pl.pallas_call(kernel, name='layer', out_shape=jax.ShapeDtypeStruct((ROWS...  150 us
    unnamed x3, local copies, waits for them, and re-layouts  3.24 us

profile of v1, /device:TPU:1, one launch (start us, length us, event | category | flops | bytes accessed | tf_op | source)
XLA Modules:
  0.0 153.7 jit_solution(672667342641653020)
XLA Ops:
  0.0 0.0 copy-start
  0.0 0.9 copy-done
  1.0 0.1 constant_dynamic-slice_fusion
  1.1 0.8 copy.9
  1.8 149.5 %layer.1 = bf16[128,4096]{1,0:T(8,128)(2,1)} custom-call(bf16[128,4096]{1,0:T(8,128)(2,1)} %bitcast.9, bf16[128,4096]{1,0:T(8,128)(2,1)} %bitcast.10, f32[1,4096]{1,0:T(1,128)} %bitcast.13, bf16[2,128,1024]{2,1,0:T(8,128)(2,1)} %bitcast.11, bf16[2,128,1024]{2,1,0:T(8,128)(2,1)} %bitcast.12, s32[64,16]{1,0:T(8,128)} %bitcast.8, ...), custom_call_target="tpu_custom_call" | custom-call | flops 6400000000 | bytes 6000000 | tf_op jit(solution)/shard_map/layer/pallas_call | solution.py:405
  151.4 2.3 %copy.11 = bf16[1,128,4096]{2,1,0:T(8,128)(2,1)} copy(bf16[1,128,4096]{2,1,0:T(8,128)(2,1)} %bitcast.7) | data formatting | bytes 2097152
Async XLA Ops:
  0.0 1.0 copy-start

commit v2 on v1

--- a/solution.py
+++ b/solution.py
@@ -23,6 +23,8 @@
 PAIR = 2 * ROWS
 BLOCK = 64
 QB = PAIR // BLOCK
+PLACES = 16
+NQB = LENGTH // BLOCK
 HIDDEN = -1e30
 SCALE = math.log2(math.e) / math.sqrt(HD)
 
@@ -39,8 +41,8 @@
 
 def kernel(
     tokens, queries, gain, wk, wv, lists, cos_hbm, sin_hbm, out,
-    wbuf, nrm, tok, gn, qin, qrot, qsend, kv, cs, sn, lst, bias, tri, sbuf, obuf,
-    in_sem, own_sem, wsend, wrecv, zsend, zrecv, core_send, core_recv, osend, orecv, olocal,
+    wbuf, nrm, tok, gn, qin, qrot, qsend, kv, cs, sn, lst, qmask, spread, tri, sbuf, mbuf, pbuf, tbuf, abuf, obuf,
+    in_sem, own_sem, wsend, wrecv, zsend, zrecv, core_send, core_recv, osend, orecv,
 ):
     s = lax.axis_index("seq")
     f = lax.axis_index("fsdp")
@@ -83,7 +85,9 @@
     q_copy = pltpu.make_async_copy(queries, qin, in_sem.at[2])
     cos_copy = pltpu.make_async_copy(cos_hbm.at[pos, :], cs.at[0], in_sem.at[3])
     sin_copy = pltpu.make_async_copy(sin_hbm.at[pos, :], sn.at[0], in_sem.at[4])
-    list_copy = pltpu.make_async_copy(lists, lst, in_sem.at[5])
+    list_copy = pltpu.make_async_copy(
+        lists.at[pl.ds(c * KVL * GROUP, KVL * GROUP)], lst, in_sem.at[5]
+    )
 
     start_own(0)
     start_own(1)
@@ -114,8 +118,8 @@
             return wbuf.at[t, (x, xn, x2, xp)[step], y, 0]
         return wbuf.at[t, x, (y, yn, y2, yp)[step], 1]
 
-    def line(t, half, step, part=None):
-        some = pl.ds(0, 4) if part is None else pl.ds(2 * part, 2)
+    def line(t, half, step, part):
+        some = pl.ds(2 * part, 2)
         if half == 0:
             return wbuf.at[t, some, (y, yn, y2, yp)[step], 0]
         return wbuf.at[t, (x, xn, x2, xp)[step], some, 1]
@@ -146,18 +150,22 @@
             for d in range(2):
                 w_wait(t, 1, half, d, rows_of(piece(t, half, 2), d))
             for d in range(2):
-                w_send(t, 2, half, d, line(t, half, 0), second_dev[half][d])
+                w_send(t, 2, half, d, line(t, half, 0, d), second_dev[half][d])
+        for half in range(2):
+            for d in range(2):
+                w_send(t, 3, half, d, line(t, half, 0, 1 - d), second_dev[half][d])
 
     def stage3(t):
         for half in range(2):
             for d, step in ((0, 1), (1, 3)):
-                w_wait(t, 2, half, d, line(t, half, step))
-                w_send(t, 3, half, d, line(t, half, step, d), second_dev[half][d])
+                w_wait(t, 2, half, d, line(t, half, step, d))
+                w_send(t, 4, half, d, line(t, half, step, d), second_dev[half][d])
 
     def stage4(t):
         for half in range(2):
-            for d in range(2):
-                w_wait(t, 3, half, d, line(t, half, 2, d))
+            for d, step in ((0, 1), (1, 3)):
+                w_wait(t, 3, half, d, line(t, half, step, 1 - d))
+                w_wait(t, 4, half, d, line(t, half, 2, d))
 
     def z_slot(t, stage, d):
         if stage == 3:
@@ -224,89 +232,115 @@
 
         q_rot_copy.start()
 
-    def make_bias():
+    def make_masks():
         list_copy.wait()
-
-        @pl.loop(0, NZ)
-        def _(r):
-            chip = lax.rem(z - r + NZ, NZ)
-            blocks = lax.div(lax.broadcasted_iota(jnp.int32, (1, PAIR), 1), BLOCK) + chip * QB
-            for n in range(KVL * GROUP * QB // 8):
-                ids = lst[8 * n : 8 * n + 8, :]
-                hit = ids[:, 0:1] == blocks
-                for slot in range(1, ids.shape[1]):
-                    hit = hit | (ids[:, slot : slot + 1] == blocks)
-                bias[8 * n : 8 * n + 8, pl.ds(pl.multiple_of(r * PAIR, PAIR), PAIR)] = jnp.where(
-                    hit, 0.0, HIDDEN
-                )
-
+        shape = (8, NQB)
+        row, lane = (lax.broadcasted_iota(jnp.int32, shape, d) for d in (0, 1))
+        mine = (lane == z * QB + row).astype(jnp.bfloat16)
+        ids = lst[...].reshape(KVL * GROUP * PLACES, NQB).astype(jnp.float32).astype(jnp.bfloat16)
+        picked = lax.dot_general(mine, ids, (((1,), (1,)), ((), ())), preferred_element_type=jnp.float32)
+        number = lax.broadcasted_iota(jnp.int32, (8, HD), 1).astype(jnp.float32)
+        for h in range(KVL * GROUP):
+            hit = picked[:, h * PLACES : h * PLACES + 1] == number
+            for place in range(1, PLACES):
+                at = h * PLACES + place
+                hit = hit | (picked[:, at : at + 1] == number)
+            hide = jnp.where(hit, 0.0, HIDDEN)
+            for b in range(QB):
+                qmask[h, b * BLOCK : (b + 1) * BLOCK, :] = jnp.broadcast_to(
+                    hide[b : b + 1, :], (BLOCK, HD)
+                ).astype(jnp.bfloat16)
+        i = lax.broadcasted_iota(jnp.int32, (PAIR, HD), 0)
+        j = lax.broadcasted_iota(jnp.int32, (PAIR, HD), 1)
+        for r in range(NZ):
+            block = lax.rem(z - r + NZ, NZ) * QB + lax.div(i, BLOCK)
+            spread[r] = (block == j).astype(jnp.float32).astype(jnp.bfloat16)
         i = lax.broadcasted_iota(jnp.int32, (PAIR, PAIR), 0)
         j = lax.broadcasted_iota(jnp.int32, (PAIR, PAIR), 1)
         tri[...] = jnp.where(j <= i, 0.0, HIDDEN)
 
     def project(t):
-        def step(k, acc):
-            kx, ky = lax.div(k, 2), lax.rem(k, 2)
-            w = wbuf[t, kx, pl.ds(2 * ky, 2)].reshape(512, HD)
-            a = nrm[:, pl.ds(pl.multiple_of(k * 512, 512), 512)]
-            return acc + jnp.dot(a, w, preferred_element_type=jnp.float32)
-
-        acc = lax.fori_loop(0, 8, step, jnp.zeros((PAIR, HD), jnp.float32))
+        acc = jnp.dot(nrm[...], wbuf[t].reshape(D, HD), preferred_element_type=jnp.float32)
         kind = lax.rem(t, 2)
         kv[t, 0] = (acc * cs[kind] + pltpu.roll(acc, HD // 2, 1) * sn[kind]).astype(jnp.bfloat16)
 
-    def attend(kvl, g):
-        q = qrot[kvl, g]
-        head = kvl * GROUP + g
+    def score(u, at):
+        kvl, g = lax.div(u, GROUP), lax.rem(u, GROUP)
+        q = jnp.concatenate([qrot[kvl, g], qmask[u]], 1)
         top = None
         for r in range(NZ):
-            scores = lax.dot_general(
-                q, kv[2 * kvl, r], (((1,), (1,)), ((), ())), preferred_element_type=jnp.float32
-            )
-            cols = slice(r * PAIR, (r + 1) * PAIR)
-            hide = jnp.concatenate(
-                [
-                    jnp.broadcast_to(bias[pl.ds(head * QB + b, 1), cols], (BLOCK, PAIR))
-                    for b in range(QB)
-                ],
-                0,
-            )
-            scores = scores * SCALE + hide
+            keys = jnp.concatenate([kv[2 * kvl, r], spread[r]], 1)
+            scores = lax.dot_general(q, keys, (((1,), (1,)), ((), ())), preferred_element_type=jnp.float32)
             if r == 0:
                 scores = scores + tri[...]
-            sbuf[:, cols] = scores
+            sbuf[at, :, r * PAIR : (r + 1) * PAIR] = scores
             here = jnp.maximum(scores[:, :HD], scores[:, HD:])
             top = here if top is None else jnp.maximum(top, here)
-        top = jnp.max(top, axis=-1, keepdims=True)
-        total, acc = None, None
-        for r in range(NZ):
-            p = jnp.exp2(sbuf[:, r * PAIR : (r + 1) * PAIR] - top)
-            both = p[:, :HD] + p[:, HD:]
-            total = both if total is None else total + both
-            part = jnp.dot(p.astype(jnp.bfloat16), kv[2 * kvl + 1, r], preferred_element_type=jnp.float32)
-            acc = part if acc is None else acc + part
-        total = jnp.sum(total, axis=-1, keepdims=True)
-        obuf[kvl, g] = (acc / total).astype(jnp.bfloat16)
+        mbuf[at] = jnp.broadcast_to(jnp.max(top, axis=-1, keepdims=True), (PAIR, HD))
+
+    def soften(u, at):
+        g = lax.rem(u, GROUP)
+        top, total = mbuf[at], None
+        for r in range(LENGTH // HD):
+            cols = slice(r * HD, (r + 1) * HD)
+            p = jnp.exp2((sbuf[at, :, cols] - top) * SCALE)
+            total = p if total is None else total + p
+            pbuf[g, :, cols] = p.astype(jnp.bfloat16)
+        tbuf[g] = jnp.broadcast_to(jnp.sum(total, axis=-1, keepdims=True), (PAIR, HD))
+
+    def weigh(u):
+        kvl, g = lax.div(u, GROUP), lax.rem(u, GROUP)
+        values = kv[2 * kvl + 1].reshape(LENGTH, HD)
+        acc = jnp.dot(pbuf[g], values, preferred_element_type=jnp.float32)
+        abuf[g] = acc / tbuf[g]
+        obuf[kvl, g] = abuf[g, pl.ds(row1, ROWS), :].astype(jnp.bfloat16)
+        cols = pl.ds(pl.multiple_of((c * KVL * GROUP + u) * HD, HD), HD)
+        out[:, cols] = abuf[g, pl.ds(row0, ROWS), :].astype(jnp.bfloat16)
 
     def out_cols(core, kvl, g):
         return out.at[:, pl.ds(pl.multiple_of(((core * KVL + kvl) * GROUP + g) * HD, HD), HD)]
 
-    def out_local(kvl, g):
-        return pltpu.make_async_copy(
-            obuf.at[kvl, g, pl.ds(row0, ROWS), :], out_cols(c, kvl, g), olocal.at[kvl, g]
-        )
-
     def out_remote(kvl, g):
         return remote(
-            obuf.at[kvl, g, pl.ds(row1, ROWS), :], out_cols(c, kvl, g), osend.at[kvl, g], orecv.at[kvl, g], partner
+            obuf.at[kvl, g], out_cols(c, kvl, g), osend.at[kvl, g], orecv.at[kvl, g], partner
         )
 
-    def attend_and_send(kvl, g):
-        attend(kvl, g)
-        out_local(kvl, g).start()
-        out_remote(kvl, g).start()
-
-    stage0(jnp.int32(0))
+    def pair_scores(m):
+        for i in range(2):
+            score(2 * m + i, i)
+        for i in range(2):
+            soften(2 * m + i, i)
+
+    def pair_values(m):
+        for i in range(2):
+            weigh(2 * m + i)
+        for i in range(2):
+            u = 2 * m + i
+            out_remote(lax.div(u, GROUP), lax.rem(u, GROUP)).start()
+
+    def around(stage):
+        def step(t):
+            z_wait(t, stage - 1)
+            if stage < 4:
+                z_send(t, stage)
+
+        return step
+
+    def compute(t):
+        stage4(t)
+
+        @pl.when(t == 0)
+        def _():
+            remote(nrm_landing, nrm_landing, core_send.at[0], core_recv.at[0], partner).wait_recv()
+
+        project(t)
+        z_send(t, 0)
+
+    for t in range(4):
+        stage0(t)
+    normalise()
+    for t in range(2):
+        stage1(t)
 
     def slot(n, carry):
         def when(t, what, low=0, high=CHUNKS):
@@ -314,65 +348,40 @@
             def _():
                 what(t)
 
-        when(n + 1, stage0)
+        when(n + 4, stage0)
+        when(n - 1, stage3)
+        when(n + 2, stage1, 2)
+        when(n - 6, pair_values)
+        when(n - 3, around(2))
+        when(n, stage2)
 
         @pl.when(n == 0)
         def _():
-            normalise()
-
-        when(n, stage1)
-
-        @pl.when(n == 0)
-        def _():
             rotate_queries()
 
-        def z1(t):
-            z_wait(t, 0)
-            z_send(t, 1)
-
-        def z2(t):
-            z_wait(t, 1)
-            z_send(t, 2)
-
-        def z3(t):
-            z_wait(t, 2)
-            z_send(t, 3)
-
-        def unit(which):
-            u = 2 * (n - 6) + which
-
-            @pl.when((u >= 0) & (u < KVL * GROUP))
-            def _():
-                attend_and_send(lax.div(u, GROUP), lax.rem(u, GROUP))
-
-        when(n - 4, z1)
-        when(n - 1, stage2)
-        when(n - 5, lambda t: z_wait(t, 3))
-        unit(0)
-        when(n - 4, z2)
-
         @pl.when(n == 1)
         def _():
-            make_bias()
-
-        when(n - 2, stage3)
-        unit(1)
-        when(n - 4, z3)
-
-        @pl.when(n == 2)
-        def _():
-            remote(nrm_landing, nrm_landing, core_send.at[0], core_recv.at[0], partner).wait_recv()
+            make_masks()
+
+        @pl.when(n == 5)
+        def _():
             remote(q_landing, q_landing, core_send.at[1], core_recv.at[1], partner).wait_recv()
 
-        def compute(t):
-            stage4(t)
-            project(t)
-            z_send(t, 0)
-
-        when(n - 3, compute)
+        when(n - 5, pair_scores)
+        when(n - 2, around(1))
+        when(n - 1, compute)
+        when(n - 4, around(4))
+        when(n - 3, around(3))
         return carry
 
-    lax.fori_loop(0, 14, slot, 0)
+    lax.fori_loop(0, 11, slot, 0)
+
+    pair_values(5)
+    pair_scores(6)
+    pair_scores(7)
+    around(4)(7)
+    pair_values(6)
+    pair_values(7)
 
     nrm_copy.wait_send()
     q_rot_copy.wait_send()
@@ -387,27 +396,22 @@
     @pl.loop(0, KVL * GROUP)
     def _(u):
         kvl, g = lax.div(u, GROUP), lax.rem(u, GROUP)
-        out_local(kvl, g).wait()
         out_remote(kvl, g).wait_send()
         theirs = out_cols(1 - c, kvl, g)
         remote(theirs, theirs, osend.at[kvl, g], orecv.at[kvl, g], partner).wait_recv()
 
 
 def on_device(tokens, queries, norm_gain, w_key, w_value, block_list):
-    s = lax.axis_index("seq")
-    c, z = lax.rem(s, 2), lax.div(s, 2)
     heads = KVL * GROUP
-    lists = lax.dynamic_slice(block_list[0], (c * heads, z * QB, 0), (heads, QB, block_list.shape[3]))
-    lists = lists.reshape(heads * QB, block_list.shape[3])
     cosine, sine = rotary_tables()
     bf16, f32 = jnp.bfloat16, jnp.float32
     dma = pltpu.SemaphoreType.DMA
     out = pl.pallas_call(
         kernel,
         name="layer",
-        out_shape=jax.ShapeDtypeStruct((ROWS, D), bf16),
+        out_shape=pltpu.VMEM((ROWS, D), bf16),
         in_specs=[pl.BlockSpec(memory_space=pl.ANY)] * 8,
-        out_specs=pl.BlockSpec(memory_space=pl.ANY),
+        out_specs=pl.BlockSpec(memory_space=pltpu.VMEM),
         scratch_shapes=[
             pltpu.VMEM((CHUNKS, NX, NY, 2, 128, HD), bf16),
             pltpu.VMEM((PAIR, D), bf16),
@@ -419,20 +423,24 @@
             pltpu.VMEM((CHUNKS, NZ, PAIR, HD), bf16),
             pltpu.VMEM((2, PAIR, HD), f32),
             pltpu.VMEM((2, PAIR, HD), f32),
-            pltpu.VMEM((heads * QB, block_list.shape[3]), jnp.int32),
-            pltpu.VMEM((heads * QB, LENGTH), f32),
+            pltpu.VMEM((heads, PLACES, NQB), jnp.int32),
+            pltpu.VMEM((heads, PAIR, HD), bf16),
+            pltpu.VMEM((NZ, PAIR, HD), bf16),
             pltpu.VMEM((PAIR, PAIR), f32),
-            pltpu.VMEM((PAIR, LENGTH), f32),
-            pltpu.VMEM((KVL, GROUP, PAIR, HD), bf16),
+            pltpu.VMEM((2, PAIR, LENGTH), f32),
+            pltpu.VMEM((2, PAIR, HD), f32),
+            pltpu.VMEM((GROUP, PAIR, LENGTH), bf16),
+            pltpu.VMEM((GROUP, PAIR, HD), f32),
+            pltpu.VMEM((GROUP, PAIR, HD), f32),
+            pltpu.VMEM((KVL, GROUP, ROWS, HD), bf16),
             dma((6,)),
             dma((CHUNKS,)),
             dma((CHUNKS,)),
-            dma((CHUNKS, 4, 2, 2)),
+            dma((CHUNKS, 5, 2, 2)),
             dma((CHUNKS,)),
             dma((CHUNKS, 4, 2)),
             dma((2,)),
             dma((2,)),
-            dma((KVL, GROUP)),
             dma((KVL, GROUP)),
             dma((KVL, GROUP)),
         ],
@@ -448,7 +456,7 @@
         norm_gain[None],
         w_key.reshape(2, 128, w_key.shape[1]),
         w_value.reshape(2, 128, w_value.shape[1]),
-        lists,
+        block_list[0].transpose(0, 2, 1),
         jnp.asarray(cosine),
         jnp.asarray(sine),
     )

time: 154 us -> 89.7 us (0.58)
  Pallas kernels: 150 us -> 88.6 us
  local copies, waits for them, and re-layouts: 4.11 us -> 0.97 us
    pallas_call x1, Pallas kernels: 150 us -> 88.6 us  [on_device(): pl.pallas_call(kernel, name='layer', out_shape=pltpu.VMEM((ROWS, D), bf16...]
    unnamed x3 -> x1, local copies, waits for them, and re-layouts: 3.24 us -> 0.97 us
where the time goes in v2:
time: 89.7 us; the launch traced here: 89.6 us
  Pallas kernels  88.6 us (99%)
  local copies, waits for them, and re-layouts  0.97 us (1%)
    pallas_call x1, Pallas kernels, on_device(): pl.pallas_call(kernel, name='layer', out_shape=pltpu.VMEM((ROWS, D), bf16...  88.6 us

profile of v2, /device:TPU:1, one launch (start us, length us, event | category | flops | bytes accessed | tf_op | source)
XLA Modules:
  0.0 89.6 jit_solution(15496513299831697536)
XLA Ops:
  0.0 88.6 %layer.1 = bf16[128,4096]{1,0:T(8,128)(2,1)S(1)} custom-call(bf16[128,4096]{1,0:T(8,128)(2,1)} %bitcast.10, bf16[128,4096]{1,0:T(8,128)(2,1)} %bitcast.11, f32[1,4096]{1,0:T(1,128)} %bitcast.15, bf16[2,128,1024]{2,1,0:T(8,128)(2,1)} %bitcast.12, bf16[2,128,1024]{2,1,0:T(8,128)(2,1)} %bitcast.13, s32[32,16,32]{2,1,0:T(8,128)} %bitcast.14, ...), custom_call_target="tpu_custom_call" | custom-call | flops 6400000000 | bytes 6000000 | tf_op jit(solution)/shard_map/layer/pallas_call | solution.py:409
  88.6 1.0 %copy.10 = bf16[1,128,4096]{2,1,0:T(8,128)(2,1)} copy(bf16[1,128,4096]{2,1,0:T(8,128)(2,1)S(1)} %bitcast.9) | data formatting | bytes 2097152

commit v3 on v2

--- a/solution.py
+++ b/solution.py
@@ -177,16 +177,57 @@
             return kv.at[t, 3 if d == 0 else 5, pl.ds(128 * d, 128), :]
         return kv.at[t, stage if d == 0 else (8 - stage) % 8]
 
+    def arrives(stage, d, chip):
+        if d == 0:
+            return chip >= stage + 1
+        return (chip + stage + 1 < NZ // 2) | (chip + stage + 1 >= NZ)
+
+    def leaves(stage, d):
+        if d == 0:
+            return (z < NZ - 1) & (z >= stage)
+        return arrives(stage, d, lax.rem(z + NZ - 1, NZ))
+
     def z_send(t, stage):
         for d in range(2):
-            remote(
-                z_source(t, stage, d), z_slot(t, stage, d), zsend.at[t], zrecv.at[t, stage, d], z_dev[d]
-            ).start()
+
+            @pl.when(leaves(stage, d))
+            def _():
+                remote(
+                    z_source(t, stage, d), z_slot(t, stage, d), zsend.at[t], zrecv.at[t, stage, d], z_dev[d]
+                ).start()
 
     def z_wait(t, stage):
         for d in range(2):
-            ref = z_slot(t, stage, d)
-            remote(ref, ref, zsend.at[t], zrecv.at[t, stage, d], partner).wait_recv()
+
+            @pl.when(arrives(stage, d, z))
+            def _():
+                ref = z_slot(t, stage, d)
+                remote(ref, ref, zsend.at[t], zrecv.at[t, stage, d], partner).wait_recv()
+
+    def z_sent(t):
+        refs = {
+            5: wbuf.at[pl.ds(0, 5), 0, 0, 0],
+            7: wbuf.at[pl.ds(0, 7), 0, 0, 0],
+            8: wbuf.at[pl.ds(0, 8), 0, 0, 0],
+            9: qsend.at[pl.ds(0, 3), pl.ds(0, 3)],
+            10: spread.at[pl.ds(0, 5)],
+        }
+        for units, chips in ((5, (7,)), (7, (4,)), (8, (5,)), (9, (0, 3)), (10, (1, 2, 6))):
+            here = functools.reduce(jnp.logical_or, [z == chip for chip in chips])
+
+            @pl.when(here)
+            def _():
+                pltpu.make_async_copy(refs[units], refs[units], zsend.at[t]).wait()
+
+    def clear_rest():
+        for r in range(1, NZ):
+            used = arrives(r - 1, 0, z) if r <= NZ // 2 else arrives(NZ - 1 - r, 1, z)
+
+            @pl.when(jnp.logical_not(used))
+            def _():
+                @pl.loop(0, CHUNKS)
+                def _(t):
+                    kv[t, r] = jnp.zeros((PAIR, HD), jnp.bfloat16)
 
     nrm_copy = remote(
         nrm.at[pl.ds(row0, ROWS), :], nrm.at[pl.ds(row0, ROWS), :], core_send.at[0], core_recv.at[0], partner
@@ -279,20 +320,21 @@
         mbuf[at] = jnp.broadcast_to(jnp.max(top, axis=-1, keepdims=True), (PAIR, HD))
 
     def soften(u, at):
-        g = lax.rem(u, GROUP)
+        place = lax.rem(u, 2 * GROUP)
         top, total = mbuf[at], None
         for r in range(LENGTH // HD):
             cols = slice(r * HD, (r + 1) * HD)
             p = jnp.exp2((sbuf[at, :, cols] - top) * SCALE)
             total = p if total is None else total + p
-            pbuf[g, :, cols] = p.astype(jnp.bfloat16)
-        tbuf[g] = jnp.broadcast_to(jnp.sum(total, axis=-1, keepdims=True), (PAIR, HD))
+            pbuf[place, :, cols] = p.astype(jnp.bfloat16)
+        tbuf[place] = jnp.broadcast_to(jnp.sum(total, axis=-1, keepdims=True), (PAIR, HD))
 
     def weigh(u):
         kvl, g = lax.div(u, GROUP), lax.rem(u, GROUP)
         values = kv[2 * kvl + 1].reshape(LENGTH, HD)
-        acc = jnp.dot(pbuf[g], values, preferred_element_type=jnp.float32)
-        abuf[g] = acc / tbuf[g]
+        place = lax.rem(u, 2 * GROUP)
+        acc = jnp.dot(pbuf[place], values, preferred_element_type=jnp.float32)
+        abuf[g] = acc / tbuf[place]
         obuf[kvl, g] = abuf[g, pl.ds(row1, ROWS), :].astype(jnp.bfloat16)
         cols = pl.ds(pl.multiple_of((c * KVL * GROUP + u) * HD, HD), HD)
         out[:, cols] = abuf[g, pl.ds(row0, ROWS), :].astype(jnp.bfloat16)
@@ -336,11 +378,13 @@
         project(t)
         z_send(t, 0)
 
-    for t in range(4):
+    for t in range(6):
         stage0(t)
     normalise()
+    for t in range(6):
+        stage1(t)
     for t in range(2):
-        stage1(t)
+        stage2(t)
 
     def slot(n, carry):
         def when(t, what, low=0, high=CHUNKS):
@@ -348,12 +392,13 @@
             def _():
                 what(t)
 
-        when(n + 4, stage0)
-        when(n - 1, stage3)
-        when(n + 2, stage1, 2)
-        when(n - 6, pair_values)
-        when(n - 3, around(2))
-        when(n, stage2)
+        when(n + 6, stage0)
+        when(n - 4, around(2))
+        when(n, stage3)
+        when(n - 5, around(3))
+        when(n - 1, compute)
+        when(n - 6, around(4))
+        when(n + 2, stage2)
 
         @pl.when(n == 0)
         def _():
@@ -362,26 +407,40 @@
         @pl.when(n == 1)
         def _():
             make_masks()
+            clear_rest()
 
         @pl.when(n == 5)
         def _():
             remote(q_landing, q_landing, core_send.at[1], core_recv.at[1], partner).wait_recv()
 
-        when(n - 5, pair_scores)
+        when(n - 6, pair_scores)
+        when(n + 6, stage1)
         when(n - 2, around(1))
-        when(n - 1, compute)
-        when(n - 4, around(4))
-        when(n - 3, around(3))
         return carry
 
-    lax.fori_loop(0, 11, slot, 0)
-
-    pair_values(5)
-    pair_scores(6)
-    pair_scores(7)
+    lax.fori_loop(0, 9, slot, 0)
+
+    around(2)(5)
+    pl.loop(0, 2)(pair_values)
+    around(3)(4)
+    around(4)(3)
+    pair_scores(3)
+    around(1)(7)
+    pl.loop(2, 4)(pair_values)
+    around(2)(6)
+    around(3)(5)
+    around(4)(4)
+    pair_scores(4)
+    around(2)(7)
+    pair_scores(5)
+    around(3)(6)
+    around(4)(5)
+    pl.loop(4, 6)(pair_values)
+    around(3)(7)
+    around(4)(6)
+    pl.loop(6, 8)(pair_scores)
     around(4)(7)
-    pair_values(6)
-    pair_values(7)
+    pl.loop(6, 8)(pair_values)
 
     nrm_copy.wait_send()
     q_rot_copy.wait_send()
@@ -390,8 +449,7 @@
     def _(t):
         sent = nrm.at[:, pl.ds(0, 15 * HD)]
         pltpu.make_async_copy(sent, sent, wsend.at[t]).wait()
-        around = kv.at[t, pl.ds(0, 7)]
-        pltpu.make_async_copy(around, around, zsend.at[t]).wait()
+        z_sent(t)
 
     @pl.loop(0, KVL * GROUP)
     def _(u):
@@ -429,8 +487,8 @@
             pltpu.VMEM((PAIR, PAIR), f32),
             pltpu.VMEM((2, PAIR, LENGTH), f32),
             pltpu.VMEM((2, PAIR, HD), f32),
-            pltpu.VMEM((GROUP, PAIR, LENGTH), bf16),
-            pltpu.VMEM((GROUP, PAIR, HD), f32),
+            pltpu.VMEM((2 * GROUP, PAIR, LENGTH), bf16),
+            pltpu.VMEM((2 * GROUP, PAIR, HD), f32),
             pltpu.VMEM((GROUP, PAIR, HD), f32),
             pltpu.VMEM((KVL, GROUP, ROWS, HD), bf16),
             dma((6,)),

time: 89.7 us -> 80.1 us (0.89)
  the two profiles are of different devices: /device:TPU:1 before, /device:TPU:193 now
where the time goes in v3:
time: 80.1 us; the launch traced here: 80 us
  Pallas kernels  79 us (99%)
  local copies, waits for them, and re-layouts  0.97 us (1%)
    pallas_call x1, Pallas kernels, on_device(): pl.pallas_call(kernel, name='layer', out_shape=pltpu.VMEM((ROWS, D), bf16...  79 us

profile of v3, /device:TPU:193, one launch (start us, length us, event | category | flops | bytes accessed | tf_op | source)
XLA Modules:
  0.0 80.0 jit_solution(2556488284861700329)
XLA Ops:
  0.0 79.0 %layer.1 = bf16[128,4096]{1,0:T(8,128)(2,1)S(1)} custom-call(bf16[128,4096]{1,0:T(8,128)(2,1)} %bitcast.10, bf16[128,4096]{1,0:T(8,128)(2,1)} %bitcast.11, f32[1,4096]{1,0:T(1,128)} %bitcast.15, bf16[2,128,1024]{2,1,0:T(8,128)(2,1)} %bitcast.12, bf16[2,128,1024]{2,1,0:T(8,128)(2,1)} %bitcast.13, s32[32,16,32]{2,1,0:T(8,128)} %bitcast.14, ...), custom_call_target="tpu_custom_call" | custom-call | flops 6400000000 | bytes 6000000 | tf_op jit(solution)/shard_map/layer/pallas_call | solution.py:467
  79.1 1.0 %copy.10 = bf16[1,128,4096]{2,1,0:T(8,128)(2,1)} copy(bf16[1,128,4096]{2,1,0:T(8,128)(2,1)S(1)} %bitcast.9) | data formatting | bytes 2097152

commit v4 on v3

--- a/solution.py
+++ b/solution.py
@@ -334,7 +334,11 @@
         values = kv[2 * kvl + 1].reshape(LENGTH, HD)
         place = lax.rem(u, 2 * GROUP)
         acc = jnp.dot(pbuf[place], values, preferred_element_type=jnp.float32)
-        abuf[g] = acc / tbuf[place]
+        put(u, acc)
+
+    def put(u, acc):
+        kvl, g = lax.div(u, GROUP), lax.rem(u, GROUP)
+        abuf[g] = acc / tbuf[lax.rem(u, 2 * GROUP)]
         obuf[kvl, g] = abuf[g, pl.ds(row1, ROWS), :].astype(jnp.bfloat16)
         cols = pl.ds(pl.multiple_of((c * KVL * GROUP + u) * HD, HD), HD)
         out[:, cols] = abuf[g, pl.ds(row0, ROWS), :].astype(jnp.bfloat16)
@@ -352,6 +356,28 @@
             score(2 * m + i, i)
         for i in range(2):
             soften(2 * m + i, i)
+
+    def pair_values_first(m):
+        for i in range(2):
+            u = 2 * m + i
+            kvl, g, place = u // GROUP, u % GROUP, u % (2 * GROUP)
+            acc = None
+            for low, high in ((0, NZ // 2), (NZ // 2 + 1, NZ)):
+                values = kv[2 * kvl + 1, low:high].reshape((high - low) * PAIR, HD)
+                weights = pbuf[place, :, low * PAIR : high * PAIR]
+                part = jnp.dot(weights, values, preferred_element_type=jnp.float32)
+                acc = part if acc is None else acc + part
+            abuf[g] = acc
+
+    def pair_values_last(m):
+        for i in range(2):
+            u = 2 * m + i
+            kvl, g, place = u // GROUP, u % GROUP, u % (2 * GROUP)
+            half = NZ // 2
+            weights = pbuf[place, :, half * PAIR : (half + 1) * PAIR]
+            part = jnp.dot(weights, kv[2 * kvl + 1, half], preferred_element_type=jnp.float32)
+            put(u, abuf[g] + part)
+            out_remote(kvl, g).start()
 
     def pair_values(m):
         for i in range(2):
@@ -378,13 +404,19 @@
         project(t)
         z_send(t, 0)
 
-    for t in range(6):
-        stage0(t)
+    stage0(0)
+    stage0(1)
+    stage0(2)
+    stage0(3)
+    stage0(4)
     normalise()
-    for t in range(6):
-        stage1(t)
-    for t in range(2):
-        stage2(t)
+    stage1(0)
+    stage0(5)
+    stage0(6)
+    stage1(1)
+    stage1(2)
+    stage1(3)
+    stage2(0)
 
     def slot(n, carry):
         def when(t, what, low=0, high=CHUNKS):
@@ -392,41 +424,45 @@
             def _():
                 what(t)
 
-        when(n + 6, stage0)
-        when(n - 4, around(2))
-        when(n, stage3)
-        when(n - 5, around(3))
-        when(n - 1, compute)
-        when(n - 6, around(4))
-        when(n + 2, stage2)
+        when(n + 1, stage2)
+        when(n - 3, around(1))
 
         @pl.when(n == 0)
         def _():
             rotate_queries()
 
-        @pl.when(n == 1)
+        @pl.when(n == 3)
         def _():
             make_masks()
             clear_rest()
 
-        @pl.when(n == 5)
+        @pl.when(n == 7)
         def _():
             remote(q_landing, q_landing, core_send.at[1], core_recv.at[1], partner).wait_recv()
 
-        when(n - 6, pair_scores)
-        when(n + 6, stage1)
-        when(n - 2, around(1))
+        when(n - 7, pair_scores)
+        when(n - 4, around(2))
+        when(n - 5, around(3))
+        when(n + 7, stage0)
+        when(n, stage3)
+        when(n + 4, stage1)
+        when(n - 1, compute)
+        when(n - 6, around(4))
         return carry
 
     lax.fori_loop(0, 9, slot, 0)
 
+    pair_scores(2)
+    around(1)(6)
+    pair_values(0)
     around(2)(5)
-    pl.loop(0, 2)(pair_values)
+    pair_scores(3)
+    around(4)(3)
+    pair_values(1)
     around(3)(4)
-    around(4)(3)
-    pair_scores(3)
     around(1)(7)
-    pl.loop(2, 4)(pair_values)
+    pair_values(2)
+    pair_values(3)
     around(2)(6)
     around(3)(5)
     around(4)(4)
@@ -435,12 +471,17 @@
     pair_scores(5)
     around(3)(6)
     around(4)(5)
-    pl.loop(4, 6)(pair_values)
+    pair_values(4)
+    pair_values(5)
     around(3)(7)
     around(4)(6)
-    pl.loop(6, 8)(pair_scores)
+    pair_scores(6)
+    pair_scores(7)
     around(4)(7)
-    pl.loop(6, 8)(pair_values)
+    pair_values_first(6)
+    pair_values_last(6)
+    pair_values_first(7)
+    pair_values_last(7)
 
     nrm_copy.wait_send()
     q_rot_copy.wait_send()

time: 80.1 us -> 79.2 us (0.989)
  Pallas kernels: 79 us -> 78.1 us
    pallas_call x1, Pallas kernels: 79 us -> 78.1 us  [on_device(): pl.pallas_call(kernel, name='layer', out_shape=pltpu.VMEM((ROWS, D), bf16...]
where the time goes in v4:
time: 79.2 us; the launch traced here: 79.1 us
  Pallas kernels  78.1 us (99%)
  local copies, waits for them, and re-layouts  0.97 us (1%)
    pallas_call x1, Pallas kernels, on_device(): pl.pallas_call(kernel, name='layer', out_shape=pltpu.VMEM((ROWS, D), bf16...  78.1 us

profile of v4, /device:TPU:193, one launch (start us, length us, event | category | flops | bytes accessed | tf_op | source)
XLA Modules:
  0.0 79.1 jit_solution(15489085262620013307)
XLA Ops:
  0.0 78.1 %layer.1 = bf16[128,4096]{1,0:T(8,128)(2,1)S(1)} custom-call(bf16[128,4096]{1,0:T(8,128)(2,1)} %bitcast.10, bf16[128,4096]{1,0:T(8,128)(2,1)} %bitcast.11, f32[1,4096]{1,0:T(1,128)} %bitcast.15, bf16[2,128,1024]{2,1,0:T(8,128)(2,1)} %bitcast.12, bf16[2,128,1024]{2,1,0:T(8,128)(2,1)} %bitcast.13, s32[32,16,32]{2,1,0:T(8,128)} %bitcast.14, ...), custom_call_target="tpu_custom_call" | custom-call | flops 6400000000 | bytes 6000000 | tf_op jit(solution)/shard_map/layer/pallas_call | solution.py:508
  78.1 1.0 %copy.10 = bf16[1,128,4096]{2,1,0:T(8,128)(2,1)} copy(bf16[1,128,4096]{2,1,0:T(8,128)(2,1)S(1)} %bitcast.9) | data formatting | bytes 2097152

commit v5 on v4

--- a/solution.py
+++ b/solution.py
@@ -477,14 +477,13 @@
     around(4)(6)
     pair_scores(6)
     pair_scores(7)
-    around(4)(7)
     pair_values_first(6)
-    pair_values_last(6)
     pair_values_first(7)
-    pair_values_last(7)
-
     nrm_copy.wait_send()
     q_rot_copy.wait_send()
+    around(4)(7)
+    pair_values_last(6)
+    pair_values_last(7)
 
     @pl.loop(0, CHUNKS)
     def _(t):

time: 79.2 us -> 78.9 us (level)
  no operation moved by 1% of the time
where the time goes in v5:
time: 78.9 us; the launch traced here: 78.8 us
  Pallas kernels  77.8 us (99%)
  local copies, waits for them, and re-layouts  0.97 us (1%)
    pallas_call x1, Pallas kernels, on_device(): pl.pallas_call(kernel, name='layer', out_shape=pltpu.VMEM((ROWS, D), bf16...  77.8 us

profile of v5, /device:TPU:193, one launch (start us, length us, event | category | flops | bytes accessed | tf_op | source)
XLA Modules:
  0.0 78.8 jit_solution(1351455091336889860)
XLA Ops:
  0.0 77.8 %layer.1 = bf16[128,4096]{1,0:T(8,128)(2,1)S(1)} custom-call(bf16[128,4096]{1,0:T(8,128)(2,1)} %bitcast.10, bf16[128,4096]{1,0:T(8,128)(2,1)} %bitcast.11, f32[1,4096]{1,0:T(1,128)} %bitcast.15, bf16[2,128,1024]{2,1,0:T(8,128)(2,1)} %bitcast.12, bf16[2,128,1024]{2,1,0:T(8,128)(2,1)} %bitcast.13, s32[32,16,32]{2,1,0:T(8,128)} %bitcast.14, ...), custom_call_target="tpu_custom_call" | custom-call | flops 6400000000 | bytes 6000000 | tf_op jit(solution)/shard_map/layer/pallas_call | solution.py:507
  77.9 1.0 %copy.10 = bf16[1,128,4096]{2,1,0:T(8,128)(2,1)} copy(bf16[1,128,4096]{2,1,0:T(8,128)(2,1)S(1)} %bitcast.9) | data formatting | bytes 2097152
